TPU v7x, 32 devices: a whole 2x2x4 slice. The times are simulated.
32 devices in a mesh: groups: 2 (over y), blk: 4 (over z), rep: 2 (over x), sub: 2 (over core).
Axes of the slice: x: 2, y: 2, z: 4, core: 2. Of those that a mesh axis runs over, the one named last changes fastest.
Arguments:
- out_grad: bfloat16 [16384, 256], P(('groups', 'blk', 'rep', 'sub')), parts along dimension 0, may hold values from -6 to 6
- pre_act: bfloat16 [16384, 256], P(('groups', 'blk', 'rep', 'sub')), parts along dimension 0, may hold values from -6 to 6
- features: bfloat16 [16384, 256], P(('groups', 'blk', 'rep', 'sub')), parts along dimension 0, may hold values from -0.15625 to 0.15625
- weight: bfloat16 [256, 256], replicated, may hold values from -0.375 to 0.375
- prop_tiles: bfloat16 [2048, 128, 128], P(('groups', 'blk', 'rep', 'sub')), parts along dimension 0, may hold values from -0.21875 to 0.21875
- tile_rows: int32 [2048], P(('groups', 'blk', 'rep', 'sub')), parts along dimension 0, may hold values from 0 to 15, as said below
- tile_cols: int32 [2048], P(('groups', 'blk', 'rep', 'sub')), parts along dimension 0, may hold values from 0 to 3
- tile_counts: int32 [128], P(('groups', 'blk', 'rep', 'sub')), parts along dimension 0, may hold values from 1 to 16, as said below
Outputs:
- feature_gradient: bfloat16 [16384, 256], P(('groups', 'blk', 'rep', 'sub')), parts along dimension 0
- grad_weight: float32 [512, 256], P('groups'), parts along dimension 0
There are 2 independent parts, one for each index of `groups`. A program takes and returns all parts, laid end to end along the dimension named above; an argument that names none is the same for every part. Nothing has to cross between parts.
Inputs may be any that keep to these rules, and one draw needn't show every extreme that they name: Within each group of 16 slots the pairs (tile_rows, tile_cols) differ. `tile_counts`: slots of a group at or beyond its count are ignored; every index d has a group with 16 live slots.
All inputs are finite; a program needn't handle non-finite values.
Results may differ from a plain program's by a relative error of at most 0.0051.
Values may be sent and summed in bfloat16 or wider, within the bound.
A program may use at most 64 MiB of HBM per device.

v0:
```python
import jax
import jax.numpy as jnp
from jax import lax
from jax.sharding import PartitionSpec as P

TILE = 128
CAP = 16


def add_group(running, source_block, adjacency_block, row_index, col_index, active_count):
    tile_side = adjacency_block.shape[1]
    blocks = source_block.reshape(
        source_block.shape[0] // tile_side, tile_side, source_block.shape[1]
    )
    matmul_argument = blocks[col_index]
    block_product = jnp.einsum(
        "giy,gym->gim", adjacency_block, matmul_argument, preferred_element_type=jnp.float32
    )
    live_mask = (lax.iota(jnp.int32, adjacency_block.shape[0]) < active_count).astype(jnp.float32)
    return running.at[row_index].add(block_product * live_mask[:, None, None])


def local(out_grad, pre_act, features, weight, prop_tiles, tile_rows, tile_cols, tile_counts):
    rows_dev = out_grad.shape[0]
    width = out_grad.shape[1]
    masked = jnp.where(pre_act > 0, out_grad, jnp.zeros_like(out_grad))
    members = lax.axis_size("rep") * lax.axis_size("sub")
    strip_tiles = members * rows_dev // TILE
    zeroed = jnp.zeros((strip_tiles, TILE, width), jnp.float32)
    gathered = lax.all_gather(masked, "blk", axis=0, tiled=True)
    first_group = 0 // rows_dev
    block_count = gathered.shape[0] // rows_dev

    def one_group(position, inner):
        group_index = first_group + position
        source_block = lax.dynamic_slice_in_dim(gathered, position * rows_dev, rows_dev, 0)
        adjacency_block = lax.dynamic_slice_in_dim(prop_tiles, group_index * CAP, CAP, 0)
        row_index = lax.dynamic_slice_in_dim(tile_rows, group_index * CAP, CAP, 0)
        col_index = lax.dynamic_slice_in_dim(tile_cols, group_index * CAP, CAP, 0)
        active_count = tile_counts[group_index]
        return add_group(inner, source_block, adjacency_block, row_index, col_index, active_count)

    partial_value = lax.fori_loop(0, block_count, one_group, zeroed)
    partial_value = partial_value.reshape(strip_tiles * TILE, width)
    strip_sum = lax.psum(partial_value, ("rep", "sub"))
    member_index = lax.axis_index(("rep", "sub"))
    own_rows = lax.dynamic_slice_in_dim(strip_sum, member_index * rows_dev, rows_dev, 0)
    propagated_gradient = own_rows.astype(jnp.bfloat16)
    feature_gradient = lax.dot_general(
        propagated_gradient, weight, (((1,), (1,)), ((), ())), preferred_element_type=jnp.float32
    ).astype(jnp.bfloat16)
    local_weight = lax.dot_general(
        features, propagated_gradient, (((0,), (0,)), ((), ())), preferred_element_type=jnp.float32
    )
    grad_weight = lax.psum(local_weight, ("blk", "rep", "sub"))
    return (feature_gradient, grad_weight)


def solution(mesh):
    placed = (
        P(("groups", "blk", "rep", "sub"), None),
        P(("groups", "blk", "rep", "sub"), None),
        P(("groups", "blk", "rep", "sub"), None),
        P(),
        P(("groups", "blk", "rep", "sub"), None, None),
        P(("groups", "blk", "rep", "sub")),
        P(("groups", "blk", "rep", "sub")),
        P(("groups", "blk", "rep", "sub")),
    )
    return jax.shard_map(
        local,
        mesh=mesh,
        in_specs=placed,
        out_specs=(P(("groups", "blk", "rep", "sub"), None), P("groups", None)),
        check_vma=False,
    )
```

profile of v0, /device:TPU:0, one launch (start us, length us, event | category | flops | bytes accessed | tf_op | source)
XLA Modules:
  0.0 217.2 jit_solution(450732424767484520)
XLA Ops:
  7.3 1.8 compare_select_fusion.2
  9.1 31.7 %all-gather.2.cloned.1.call-done = bf16[2048,256]{1,0:T(8,128)(2,1)} async-done(((bf16[512,256]{1,0:T(8,128)(2,1)}), bf16[2048,256]{1,0:T(8,128)(2,1)}) %all-gather.2.cloned.1.call-update) | async-done | bytes 1048592 | tf_op jit(solution)/shard_map/all_gather | solution.py:30
  40.9 1.5 broadcast_in_dim.20
  42.4 35.4 %while.13 = (s32[]{:T(128)}, f32[16,128,256]{2,1,0:T(8,128)}, s32[64]{0:T(128)S(1)}, bf16[64,128,128]{2,1,0:T(8,128)(2,1)}, bf16[2048,256]{1,0:T(8,128)(2,1)}, /...) while((s32[]{:T(128)}, f32[16,128,256]{2,1,0:T(8,128)}, ...), condition=%wide.region_2.3_spmd, body=%wide.region_0.2_spmd.sunk | while | flops 135267472 | bytes 12587837 | solution.py:43
  42.5 1.0 constant_dynamic-slice_fusion.2
  43.5 0.6 gather_fusion
  44.1 0.6 dynamic_slice.54
  44.7 0.6 compare_convert_fusion.2
  45.4 1.5 convolution_multiply_fusion.2
  46.8 4.4 %scatter_fusion = f32[16,128,256]{2,1,0:T(8,128)} fusion(f32[16,128,256]{2,1,0:T(8,128)} %get-tuple-element.206, s32[16]{0:T(128)S(1)} %get-tuple-element.190, f32[16,128,256]{2,1,0:T(8,128)S(1)} %convolution_multiply_fusion.2), kind=kCustom, calls=%fused_computation.1.clone.1 | custom fusion | flops 524288 | bytes 6291520 | tf_op jit(solution)/shard_map/while/body/eval_jaxpr/scatter-add | solution.py:20
  51.3 1.0 constant_dynamic-slice_fusion.2
  52.3 0.6 gather_fusion
  52.9 0.6 dynamic_slice.54
  53.5 0.6 compare_convert_fusion.2
  54.2 1.5 convolution_multiply_fusion.2
  55.7 4.4 %scatter_fusion = f32[16,128,256]{2,1,0:T(8,128)} fusion(f32[16,128,256]{2,1,0:T(8,128)} %get-tuple-element.206, s32[16]{0:T(128)S(1)} %get-tuple-element.190, f32[16,128,256]{2,1,0:T(8,128)S(1)} %convolution_multiply_fusion.2), kind=kCustom, calls=%fused_computation.1.clone.1 | custom fusion | flops 524288 | bytes 6291520 | tf_op jit(solution)/shard_map/while/body/eval_jaxpr/scatter-add | solution.py:20
  60.1 1.0 constant_dynamic-slice_fusion.2
  61.1 0.6 gather_fusion
  61.7 0.6 dynamic_slice.54
  62.3 0.6 compare_convert_fusion.2
  63.0 1.5 convolution_multiply_fusion.2
  64.5 4.4 %scatter_fusion = f32[16,128,256]{2,1,0:T(8,128)} fusion(f32[16,128,256]{2,1,0:T(8,128)} %get-tuple-element.206, s32[16]{0:T(128)S(1)} %get-tuple-element.190, f32[16,128,256]{2,1,0:T(8,128)S(1)} %convolution_multiply_fusion.2), kind=kCustom, calls=%fused_computation.1.clone.1 | custom fusion | flops 524288 | bytes 6291520 | tf_op jit(solution)/shard_map/while/body/eval_jaxpr/scatter-add | solution.py:20
  69.0 1.0 constant_dynamic-slice_fusion.2
  70.0 0.6 gather_fusion
  71.2 0.6 compare_convert_fusion.2
  71.8 1.5 convolution_multiply_fusion.2
  73.3 4.5 %scatter_fusion = f32[16,128,256]{2,1,0:T(8,128)} fusion(f32[16,128,256]{2,1,0:T(8,128)} %get-tuple-element.206, s32[16]{0:T(128)S(1)} %get-tuple-element.190, f32[16,128,256]{2,1,0:T(8,128)S(1)} %convolution_multiply_fusion.2), kind=kCustom, calls=%fused_computation.1.clone.1 | custom fusion | flops 524288 | bytes 6291520 | tf_op jit(solution)/shard_map/while/body/eval_jaxpr/scatter-add | solution.py:20
  77.8 42.0 %all-reduce.4 = bf16[2048,256]{1,0:T(8,128)(2,1)S(1)} all-reduce(f32[2048,256]{1,0:T(8,128)} %bitcast.15), channel_id=1, replica_groups=mesh['groups'=2,'blk'=4,'rep'=2,'sub'=2] {'rep','sub'}, use_global_device_ids=true, to_apply=%region_3.4 | all-reduce | flops 524288 | bytes 3145728 | tf_op jit(solution)/shard_map/psum | solution.py:45
  119.8 1.0 convolution_bitcast_fusion
  120.8 1.0 convolution_convert_fusion
  121.8 86.8 %all-reduce.3.cloned.1.call-done = f32[256,256]{0,1:T(8,128)} async-done(((f32[256,256]{0,1:T(8,128)}), f32[256,256]{0,1:T(8,128)}) %all-reduce.3.cloned.1.call-update) | async-done | bytes 262160 | tf_op jit(solution)/shard_map/psum | solution.py:55
  208.6 1.8 copy.10
  (23 shorter events, 1.1 us)
Async XLA Ops:
  7.2 112.7 %copy-start = (bf16[512,256]{1,0:T(8,128)(2,1)S(1)}, bf16[512,256]{1,0:T(8,128)(2,1)}, u32[]{:S(2)}) copy-start(bf16[512,256]{1,0:T(8,128)(2,1)} %param.12) | copy-start | bytes 786436
  7.2 35.2 %copy-start.2 = (s32[64]{0:T(128)S(1)}, s32[64]{0:T(128)}, u32[]{:S(2)}) copy-start(s32[64]{0:T(128)} %param.15) | copy-start | bytes 772
  7.2 35.2 %copy-start.3 = (s32[64]{0:T(128)S(1)}, s32[64]{0:T(128)}, u32[]{:S(2)}) copy-start(s32[64]{0:T(128)} %param.16) | copy-start | bytes 772
  7.2 35.2 %copy-start.4 = (s32[4]{0:T(128)S(1)}, s32[4]{0:T(128)}, u32[]{:S(2)}) copy-start(s32[4]{0:T(128)} %param.17) | copy-start | bytes 52
  7.2 33.6 %all-gather.2.cloned.1.call-start = ((), (), s32[]{:S(2)}) async-start(), calls=%async_computation | async-start | bytes 1310720 | tf_op jit(solution)/shard_map/all_gather | solution.py:30
  9.1 199.5 %all-reduce.3.cloned.1.call-start = ((), (), s32[]{:S(2)}) async-start(), calls=%async_computation.1 | async-start | bytes 524288 | tf_op jit(solution)/shard_map/psum | solution.py:55
  77.8 43.1 %copy-start.1 = (bf16[256,256]{1,0:T(8,128)(2,1)S(1)}, bf16[256,256]{1,0:T(8,128)(2,1)}, u32[]{:S(2)}) copy-start(bf16[256,256]{1,0:T(8,128)(2,1)} %param.13) | copy-start | bytes 393220
Sparse Core Ops, SparseCore 0:
  10.2 30.6 all-gather.1
  121.0 87.5 all-reduce.2
where the time goes:
time: 218 us; the launch traced here: 217 us
  waiting for transfers between devices  119 us (55%)
  blocking collectives  42 us (19%)
  other arithmetic  22.5 us (10%)
  between operations  14.1 us (6%)
  local copies, waits for them, and re-layouts  12 us (6%)
  matrix products  7.81 us (4%)
    psum x1, waiting for transfers between devices, local(): grad_weight = lax.psum(local_weight, ('blk', 'rep', 'sub'))  86.8 us
    psum x1, blocking collectives, local(): strip_sum = lax.psum(partial_value, ('rep', 'sub'))  42 us
    all_gather x1, waiting for transfers between devices, local(): gathered = lax.all_gather(masked, 'blk', axis=0, tiled=True)  31.7 us
    scatter-add x4, other arithmetic, add_group(): return running.at[row_index].add(block_product * live_mask[:, None, None])  17.8 us
    dot_general x4, matrix products, add_group(): jnp.einsum('giy,gym->gim', adjacency_block, matmul_argument, preferred_el...  5.86 us
  transfers between devices with their start and end apart: 2, of which 2 were waited for; matrix products, arithmetic and copies ran while one was open for 0% of the time, Pallas kernels for 0%

commit v1 on v0

v1 whole, which is shorter than its diff:
```python
import functools

import jax
import jax.numpy as jnp
from jax import lax
from jax.experimental import pallas as pl
from jax.experimental.pallas import tpu as pltpu
from jax.sharding import PartitionSpec as P

TILE = 128
CAP = 16
HALF = 128
MESH = pl.DeviceIdType.MESH
BF16 = jnp.bfloat16
F32 = jnp.float32
SUB_WIRE = jnp.float32
KEEP_BYTES = 16 << 20


def kernel(n, n_rep, n_sub, halves, keep,
           og, pa, tr, tc, cnt, feat_any, w_any, tiles_any,
           fg, gw,
           gath, dense, tiles, inv_v, inv_s, part, sub_out, sub_in, rep_out, rep_in, acc, prop,
           feat, w, gwl, g1_out, g1_in, zbuf, gfin,
           loc_sem, ssem, rsem, sub_ss, sub_rs, rep_ss, rep_rs, g1_ss, g1_rs, z_ss, z_rs, f_ss, f_rs):
    rows = og.shape[0]
    slots = tiles_any.shape[0]
    shard = rows // TILE
    members = n_rep * n_sub
    strip = members * rows
    strip_tiles = strip // TILE
    b = lax.axis_index("blk")
    r = lax.axis_index("rep")
    s = lax.axis_index("sub")
    m = r * n_sub + s
    piece = gwl.shape[0] // members

    def member(t):
        return {"rep": t // n_sub, "sub": lax.rem(t, n_sub)}

    barrier = pltpu.get_barrier_semaphore()
    for o in range(1, n):
        pl.semaphore_signal(barrier, inc=1, device_id={"blk": lax.rem(b + o, n)}, device_id_type=MESH)
    for o in range(1, members):
        pl.semaphore_signal(barrier, inc=1, device_id=member(lax.rem(m + o, members)), device_id_type=MESH)

    tiles_copy = pltpu.make_async_copy(tiles_any, tiles.at[pl.ds(0, slots)], loc_sem.at[0])
    feat_copy = pltpu.make_async_copy(feat_any, feat, loc_sem.at[1])
    w_copy = pltpu.make_async_copy(w_any, w, loc_sem.at[2])
    tiles_copy.start()
    feat_copy.start()
    w_copy.start()

    for c in range(halves):
        cols = pl.ds(c * HALF, HALF)
        x = og[:, cols]
        gath[b, c] = jnp.where(pa[:, cols] > 0, x, jnp.zeros_like(x))

    def block_copy(c, origin, way):
        return pltpu.make_async_remote_copy(
            src_ref=gath.at[origin, c], dst_ref=gath.at[origin, c],
            send_sem=ssem.at[way, origin, c], recv_sem=rsem.at[origin, c],
            device_id={"blk": jnp.clip(b + (1 if way else -1), 0, n - 1)}, device_id_type=MESH)

    def send(c, origin, way):
        @pl.when((b + 1 < n) if way else (b > 0))
        def _():
            block_copy(c, origin, way).start()

    pl.semaphore_wait(barrier, n - 1 + members - 1)
    send(0, b, 0)
    send(0, b, 1)

    lane = lax.broadcasted_iota(jnp.int32, (1, inv_v.shape[1]), 1)

    def invert(g, carry):
        v = jnp.full((1, inv_v.shape[1]), slots, jnp.int32)
        for k in range(CAP):
            slot = g * CAP + k
            key = jnp.where(k < cnt[g], tr[slot] * shard + tc[slot], -1)
            v = jnp.where(lane == key, slot, v)
        inv_v[pl.ds(g, 1), :] = v
        return carry

    lax.fori_loop(0, n, invert, 0)
    inv_copy = pltpu.make_async_copy(inv_v, inv_s, loc_sem.at[3])
    inv_copy.start()
    tiles[slots] = jnp.zeros((TILE, TILE), BF16)
    inv_copy.wait()
    tiles_copy.wait()

    def build(g):
        where = g if keep else 0

        def one(t, carry):
            for c in range(shard):
                index = inv_s[g, t * shard + c]
                dense[where, pl.ds(pl.multiple_of(t * TILE, TILE), TILE), pl.ds(c * TILE, TILE)] = tiles[index]
            return carry

        lax.fori_loop(0, strip_tiles, one, 0)

    def accumulate(g, c, first):
        where = g if keep else 0
        if c == 0 or not keep:
            build(g)
        step = 512

        def one(t, carry):
            at = pl.ds(pl.multiple_of(t * step, step), step)
            product = jnp.dot(dense[where, at, :], gath[g, c], preferred_element_type=F32)
            if first:
                part[c, at, :] = product
            else:
                part[c, at, :] += product
            return carry

        lax.fori_loop(0, strip // step, one, 0)

    def gather(c, low, high):
        def one(d, carry):
            @pl.when(b - d >= 0)
            def _():
                block_copy(c, b - d, 1).wait_recv()
                send(c, b - d, 1)

            @pl.when(b + d < n)
            def _():
                block_copy(c, b + d, 0).wait_recv()
                send(c, b + d, 0)

            if c + 1 < halves:
                @pl.when(d == 1)
                def _():
                    send(c + 1, b, 0)
                    send(c + 1, b, 1)

            @pl.when(b - d >= 0)
            def _():
                accumulate(b - d, c, False)

            @pl.when(b + d < n)
            def _():
                accumulate(b + d, c, False)
            return carry

        if low < high:
            lax.fori_loop(low, high, one, 0)

    def sub_copy(c, o):
        return pltpu.make_async_remote_copy(
            src_ref=sub_out.at[c, o - 1], dst_ref=sub_in.at[c, o - 1],
            send_sem=sub_ss.at[c, o - 1], recv_sem=sub_rs.at[c, o - 1],
            device_id={"sub": lax.rem(s + o, n_sub)}, device_id_type=MESH)

    def rep_copy(c, o):
        return pltpu.make_async_remote_copy(
            src_ref=rep_out.at[c, o - 1], dst_ref=rep_in.at[c, o - 1],
            send_sem=rep_ss.at[c, o - 1], recv_sem=rep_rs.at[c, o - 1],
            device_id={"rep": lax.rem(r + o, n_rep)}, device_id_type=MESH)

    def block_rows(t):
        return pl.ds(pl.multiple_of(t * rows, rows), rows)

    def sub_stage(c):
        for o in range(1, n_sub):
            t = lax.rem(s + o, n_sub)
            for q in range(n_rep):
                sub_out[c, o - 1, pl.ds(q * rows, rows), :] = part[c, block_rows(q * n_sub + t), :].astype(SUB_WIRE)
            sub_copy(c, o).start()

    def rep_stage(c):
        for o in range(1, n_sub):
            sub_copy(c, o).wait_recv()

        def summed(t):
            total = part[c, block_rows(t * n_sub + s), :]
            for o in range(1, n_sub):
                total = total + sub_in[c, o - 1, block_rows(t), :].astype(F32)
            return total

        for o in range(1, n_rep):
            rep_out[c, o - 1] = summed(lax.rem(r + o, n_rep)).astype(BF16)
            rep_copy(c, o).start()
        acc[c] = summed(r)

    def prop_stage(c):
        for o in range(1, n_rep):
            rep_copy(c, o).wait_recv()
        total = acc[c]
        for o in range(1, n_rep):
            total = total + rep_in[c, o - 1].astype(F32)
        prop[c] = total.astype(BF16)

    def weight_term(c):
        gwl[:, pl.ds(c * HALF, HALF)] = lax.dot_general(
            feat[...], prop[c], (((0,), (0,)), ((), ())), preferred_element_type=F32)

    accumulate(b, 0, True)
    gather(0, 1, n)
    for c in range(halves):
        sub_stage(c)
        if c + 1 < halves:
            accumulate(b, c + 1, True)
            gather(c + 1, 1, 2)
            rep_stage(c)
            gather(c + 1, 2, 3)
            prop_stage(c)
            if c == 0:
                feat_copy.wait()
                w_copy.wait()
            weight_term(c)
            gather(c + 1, 3, n)
        else:
            rep_stage(c)
            prop_stage(c)
            weight_term(c)

    def g1_copy(o):
        return pltpu.make_async_remote_copy(
            src_ref=g1_out.at[o - 1], dst_ref=g1_in.at[o - 1],
            send_sem=g1_ss.at[o - 1], recv_sem=g1_rs.at[o - 1],
            device_id=member(lax.rem(m + o, members)), device_id_type=MESH)

    def z_copy(o, origin):
        return pltpu.make_async_remote_copy(
            src_ref=zbuf.at[origin], dst_ref=zbuf.at[origin],
            send_sem=z_ss.at[o - 1], recv_sem=z_rs.at[origin],
            device_id={"blk": lax.rem(b + o, n)}, device_id_type=MESH)

    def f_copy(o, origin):
        return pltpu.make_async_remote_copy(
            src_ref=gfin.at[origin], dst_ref=gfin.at[origin],
            send_sem=f_ss.at[o - 1], recv_sem=f_rs.at[origin],
            device_id=member(lax.rem(m + o, members)), device_id_type=MESH)

    def piece_rows(t):
        return pl.ds(pl.multiple_of(t * piece, piece), piece)

    for o in range(1, members):
        g1_out[o - 1] = gwl[piece_rows(lax.rem(m + o, members)), :].astype(BF16)
        g1_copy(o).start()

    total = None
    for c in range(halves):
        term = lax.dot_general(prop[c], w[:, pl.ds(c * HALF, HALF)], (((1,), (1,)), ((), ())),
                               preferred_element_type=F32)
        total = term if total is None else total + term
    fg[...] = total.astype(BF16)

    for o in range(1, members):
        g1_copy(o).wait_recv()
    total = gwl[piece_rows(m), :]
    for o in range(1, members):
        total = total + g1_in[o - 1].astype(F32)
    zbuf[b] = total.astype(BF16)
    for o in range(1, n):
        z_copy(o, b).start()
    for o in range(1, n):
        z_copy(o, lax.rem(b + o, n)).wait_recv()
    total = zbuf[0].astype(F32)
    for q in range(1, n):
        total = total + zbuf[q].astype(F32)
    gfin[m] = total.astype(BF16)
    for o in range(1, members):
        f_copy(o, m).start()
    for o in range(1, members):
        f_copy(o, lax.rem(m + o, members)).wait_recv()
    for q in range(members):
        gw[pl.ds(q * piece, piece), :] = gfin[q].astype(F32)

    def drain(origin, carry):
        for c in range(halves):
            @pl.when((origin <= b) & (b + 1 < n))
            def _():
                block_copy(c, origin, 1).wait_send()

            @pl.when((origin >= b) & (b > 0))
            def _():
                block_copy(c, origin, 0).wait_send()
        return carry

    lax.fori_loop(0, n, drain, 0)
    for c in range(halves):
        for o in range(1, n_sub):
            sub_copy(c, o).wait_send()
        for o in range(1, n_rep):
            rep_copy(c, o).wait_send()
    for o in range(1, members):
        g1_copy(o).wait_send()
        f_copy(o, m).wait_send()
    for o in range(1, n):
        z_copy(o, b).wait_send()


def local(n, n_rep, n_sub, out_grad, pre_act, features, weight, prop_tiles, tile_rows, tile_cols, tile_counts):
    rows, width = out_grad.shape
    f_in = features.shape[1]
    slots = prop_tiles.shape[0]
    halves = width // HALF
    members = n_rep * n_sub
    strip = members * rows
    keep = n * strip * rows * 2 <= KEEP_BYTES
    lanes = -(-(strip // TILE) * (rows // TILE) // 128) * 128
    inv_shape = (-(-n // 8) * 8, lanes)
    piece = f_in // members
    dma = pltpu.SemaphoreType.DMA
    vmem = pl.BlockSpec(memory_space=pltpu.VMEM)
    smem = pl.BlockSpec(memory_space=pltpu.SMEM)
    hbm = pl.BlockSpec(memory_space=pl.ANY)
    subs, reps = max(n_sub - 1, 1), max(n_rep - 1, 1)
    return pl.pallas_call(
        functools.partial(kernel, n, n_rep, n_sub, halves, keep),
        out_shape=(
            jax.ShapeDtypeStruct((rows, weight.shape[0]), BF16),
            jax.ShapeDtypeStruct((f_in, width), F32),
        ),
        in_specs=[vmem, vmem, smem, smem, smem, hbm, hbm, hbm],
        out_specs=(vmem, vmem),
        scratch_shapes=[
            pltpu.VMEM((n, halves, rows, HALF), BF16),
            pltpu.VMEM((n if keep else 1, strip, rows), BF16),
            pltpu.VMEM((slots + 1, TILE, TILE), BF16),
            pltpu.VMEM(inv_shape, jnp.int32),
            pltpu.SMEM(inv_shape, jnp.int32),
            pltpu.VMEM((halves, strip, HALF), F32),
            pltpu.VMEM((halves, subs, n_rep * rows, HALF), SUB_WIRE),
            pltpu.VMEM((halves, subs, n_rep * rows, HALF), SUB_WIRE),
            pltpu.VMEM((halves, reps, rows, HALF), BF16),
            pltpu.VMEM((halves, reps, rows, HALF), BF16),
            pltpu.VMEM((halves, rows, HALF), F32),
            pltpu.VMEM((halves, rows, HALF), BF16),
            pltpu.VMEM(features.shape, BF16),
            pltpu.VMEM(weight.shape, BF16),
            pltpu.VMEM((f_in, width), F32),
            pltpu.VMEM((members - 1, piece, width), BF16),
            pltpu.VMEM((members - 1, piece, width), BF16),
            pltpu.VMEM((n, piece, width), BF16),
            pltpu.VMEM((members, piece, width), BF16),
            dma((4,)),
            dma((2, n, halves)),
            dma((n, halves)),
            dma((halves, subs)),
            dma((halves, subs)),
            dma((halves, reps)),
            dma((halves, reps)),
            dma((members - 1,)),
            dma((members - 1,)),
            dma((n - 1,)),
            dma((n,)),
            dma((members - 1,)),
            dma((members,)),
        ],
        compiler_params=pltpu.CompilerParams(
            collective_id=0, has_side_effects=True, vmem_limit_bytes=48 << 20),
    )(out_grad, pre_act, tile_rows, tile_cols, tile_counts, features, weight, prop_tiles)


def solution(mesh):
    placed = P(("groups", "blk", "rep", "sub"))
    return jax.shard_map(
        functools.partial(local, mesh.shape["blk"], mesh.shape["rep"], mesh.shape["sub"]),
        mesh=mesh,
        in_specs=(placed, placed, placed, P(), placed, placed, placed, placed),
        out_specs=(placed, P("groups", None)),
        check_vma=False,
    )
```

time: 218 us -> 55.2 us (0.25)
  waiting for transfers between devices: 119 us -> 0 us
  Pallas kernels: 0 us -> 45.6 us
  blocking collectives: 42 us -> 0 us
  other arithmetic: 22.5 us -> 0 us
  between operations: 14.1 us -> 0.66 us
  matrix products: 7.81 us -> 0 us
  local copies, waits for them, and re-layouts: 12 us -> 8.71 us
    psum x1 -> x0, waiting for transfers between devices: 86.8 us -> none  [local(): grad_weight = lax.psum(local_weight, ('blk', 'rep', 'sub'))]
    pallas_call x0 -> x1, Pallas kernels: none -> 45.6 us  [local(): pl.pallas_call(functools.partial(kernel, n, n_rep, n_sub, halves, keep),...]
    psum x1 -> x0, blocking collectives: 42 us -> none  [local(): strip_sum = lax.psum(partial_value, ('rep', 'sub'))]
    all_gather x1 -> x0, waiting for transfers between devices: 31.7 us -> none  [local(): gathered = lax.all_gather(masked, 'blk', axis=0, tiled=True)]
    scatter-add x4 -> x0, other arithmetic: 17.8 us -> none  [add_group(): return running.at[row_index].add(block_product * live_mask[:, None, None])]
    dot_general x6 -> x0, matrix products: 7.81 us -> none  [the longest x4 5.86 us: add_group(): jnp.einsum('giy,gym->gim', adjacency_block, matmul_argument, preferred_el...]
    unnamed x11 -> x18, local copies, waits for them, and re-layouts: 1.81 us -> 8.71 us
    dynamic_slice x8 -> x0, local copies, waits for them, and re-layouts: 6.23 us -> none  [the longest x4 3.87 us: one_group(): lax.dynamic_slice_in_dim(gathered, position * rows_dev, rows_dev, 0)]
  transfers between devices with their start and end apart: 2 -> 0, of which waited for: 2 -> 0; matrix products, arithmetic and copies ran while one was open for 0% -> 0% of each run, Pallas kernels for 0% -> 0%
where the time goes in v1:
time: 55.2 us; the launch traced here: 54.9 us
  Pallas kernels  45.6 us (83%)
  local copies, waits for them, and re-layouts  8.71 us (16%)
  between operations  0.66 us (1%)
    pallas_call x1, Pallas kernels, local(): pl.pallas_call(functools.partial(kernel, n, n_rep, n_sub, halves, keep),...  45.6 us
    unnamed x18, local copies, waits for them, and re-layouts  8.71 us

profile of v1, /device:TPU:0, one launch (start us, length us, event | category | flops | bytes accessed | tf_op | source)
XLA Modules:
  0.0 54.9 jit_solution(4388343028416320102)
XLA Ops:
  0.6 0.0 copy-start
  0.6 1.6 %copy-done = bf16[64,128,128]{2,1,0:T(8,128)(2,1)S(1)} copy-done((bf16[64,128,128]{2,1,0:T(8,128)(2,1)S(1)}, bf16[64,128,128]{2,1,0:T(8,128)(2,1)}, u32[]{:S(2)}) %copy-start) | copy-done | bytes 2097176
  2.2 0.0 copy-start.1
  2.2 0.9 %copy-done.1 = bf16[512,256]{1,0:T(8,128)(2,1)S(1)} copy-done((bf16[512,256]{1,0:T(8,128)(2,1)S(1)}, bf16[512,256]{1,0:T(8,128)(2,1)}, u32[]{:S(2)}) %copy-start.1) | copy-done | bytes 262168
  3.2 0.0 copy-start.2
  3.2 0.9 %copy-done.2 = bf16[512,256]{1,0:T(8,128)(2,1)S(1)} copy-done((bf16[512,256]{1,0:T(8,128)(2,1)S(1)}, bf16[512,256]{1,0:T(8,128)(2,1)}, u32[]{:S(2)}) %copy-start.2) | copy-done | bytes 262168
  4.1 0.0 copy-start.3
  4.1 0.9 %copy-done.3 = bf16[512,256]{1,0:T(8,128)(2,1)S(1)} copy-done((bf16[512,256]{1,0:T(8,128)(2,1)S(1)}, bf16[512,256]{1,0:T(8,128)(2,1)}, u32[]{:S(2)}) %copy-start.3) | copy-done | bytes 262168
  5.1 0.0 copy-start.4
  5.1 0.9 %copy-done.4 = bf16[256,256]{1,0:T(8,128)(2,1)S(1)} copy-done((bf16[256,256]{1,0:T(8,128)(2,1)S(1)}, bf16[256,256]{1,0:T(8,128)(2,1)}, u32[]{:S(2)}) %copy-start.4) | copy-done | bytes 131096
  6.0 0.0 copy-start.5
  6.0 0.7 %copy-done.5 = s32[64]{0:T(128)S(1)} copy-done((s32[64]{0:T(128)S(1)}, s32[64]{0:T(128)}, u32[]{:S(2)}) %copy-start.5) | copy-done | bytes 280
  6.6 0.0 copy-start.6
  6.6 0.7 %copy-done.6 = s32[64]{0:T(128)S(1)} copy-done((s32[64]{0:T(128)S(1)}, s32[64]{0:T(128)}, u32[]{:S(2)}) %copy-start.6) | copy-done | bytes 280
  7.3 0.0 copy-start.7
  7.3 0.7 %copy-done.7 = s32[4]{0:T(128)S(1)} copy-done((s32[4]{0:T(128)S(1)}, s32[4]{0:T(128)}, u32[]{:S(2)}) %copy-start.7) | copy-done | bytes 40
  7.9 45.6 %shard_map.95 = (bf16[512,256]{1,0:T(8,128)(2,1)S(1)}, f32[256,256]{1,0:T(8,128)S(1)}) custom-call(bf16[512,256]{1,0:T(8,128)(2,1)S(1)} %copy-done.1, bf16[512,256]{1,0:T(8,128)(2,1)S(1)} %copy-done.2, s32[64]{0:T(128)S(1)} %copy-done.5, s32[64]{0:T(128)S(1)} %copy-done.6, s32[4]{0:T(128)S(1)} %copy-done.7, bf16[512,256]{1,0:T(8,128)(2,1)S(1)} %copy-done.3, ...), custom_call_target="tpu_custom_call" | custom-call | tf_op jit(solution)/shard_map/pallas_call | solution.py:312
  53.5 0.7 %copy.12 = bf16[512,256]{1,0:T(8,128)(2,1)} copy(bf16[512,256]{1,0:T(8,128)(2,1)S(1)} %get-tuple-element.4) | data formatting | bytes 524288
  54.2 0.7 %copy.13 = f32[256,256]{1,0:T(8,128)} copy(f32[256,256]{1,0:T(8,128)S(1)} %get-tuple-element.5) | data formatting | bytes 524288
Async XLA Ops:
  0.6 1.6 %copy-start = (bf16[64,128,128]{2,1,0:T(8,128)(2,1)S(1)}, bf16[64,128,128]{2,1,0:T(8,128)(2,1)}, u32[]{:S(2)}) copy-start(bf16[64,128,128]{2,1,0:T(8,128)(2,1)} %tiles_any.1) | copy-start | bytes 6291460
  2.2 0.9 %copy-start.1 = (bf16[512,256]{1,0:T(8,128)(2,1)S(1)}, bf16[512,256]{1,0:T(8,128)(2,1)}, u32[]{:S(2)}) copy-start(bf16[512,256]{1,0:T(8,128)(2,1)} %og.1) | copy-start | bytes 786436
  3.2 0.9 %copy-start.2 = (bf16[512,256]{1,0:T(8,128)(2,1)S(1)}, bf16[512,256]{1,0:T(8,128)(2,1)}, u32[]{:S(2)}) copy-start(bf16[512,256]{1,0:T(8,128)(2,1)} %pa.1) | copy-start | bytes 786436
  4.1 0.9 %copy-start.3 = (bf16[512,256]{1,0:T(8,128)(2,1)S(1)}, bf16[512,256]{1,0:T(8,128)(2,1)}, u32[]{:S(2)}) copy-start(bf16[512,256]{1,0:T(8,128)(2,1)} %feat_any.1) | copy-start | bytes 786436
  5.1 0.9 %copy-start.4 = (bf16[256,256]{1,0:T(8,128)(2,1)S(1)}, bf16[256,256]{1,0:T(8,128)(2,1)}, u32[]{:S(2)}) copy-start(bf16[256,256]{1,0:T(8,128)(2,1)} %w_any.1) | copy-start | bytes 393220
  6.0 0.7 %copy-start.5 = (s32[64]{0:T(128)S(1)}, s32[64]{0:T(128)}, u32[]{:S(2)}) copy-start(s32[64]{0:T(128)} %tr.1) | copy-start | bytes 772
  6.6 0.7 %copy-start.6 = (s32[64]{0:T(128)S(1)}, s32[64]{0:T(128)}, u32[]{:S(2)}) copy-start(s32[64]{0:T(128)} %tc.1) | copy-start | bytes 772
  7.3 0.7 %copy-start.7 = (s32[4]{0:T(128)S(1)}, s32[4]{0:T(128)}, u32[]{:S(2)}) copy-start(s32[4]{0:T(128)} %cnt.1) | copy-start | bytes 52

commit v2 on v1

v2 whole, which is shorter than its diff:
```python
import functools

import jax
import jax.numpy as jnp
from jax import lax
from jax.experimental import pallas as pl
from jax.experimental.pallas import tpu as pltpu
from jax.sharding import PartitionSpec as P

TILE = 128
CAP = 16
HALF = 128
MESH = pl.DeviceIdType.MESH
BF16 = jnp.bfloat16
F32 = jnp.float32
SUB_WIRE = jnp.float32
G_WIRE = jnp.bfloat16
KEEP_BYTES = 16 << 20
PIECES = 2


def kernel(n, n_rep, n_sub, halves, keep,
           og_any, pa_any, tr_any, tc_any, cnt_any, feat_any, w_any, tiles_any,
           fg, gw,
           og, pa, tr, tc, cnt,
           gath, dense, tiles, inv_v, inv_s, part, sub_out, sub_in, rep_out, rep_in, acc, prop,
           feat, feat_t, w, part_b, g1_out, g1_in, zbuf, gfin,
           loc_sem, ssem, rsem, sub_ss, sub_rs, rep_ss, rep_rs, ft_ss, ft_rs, g1_ss, g1_rs, z_ss, z_rs, f_ss, f_rs):
    rows = og_any.shape[0]
    slots = tiles_any.shape[0]
    shard = rows // TILE
    members = n_rep * n_sub
    strip = members * rows
    strip_tiles = strip // TILE
    b = lax.axis_index("blk")
    r = lax.axis_index("rep")
    s = lax.axis_index("sub")
    m = r * n_sub + s
    piece = feat_any.shape[1] // members
    span = rows // PIECES

    def member(t):
        return {"rep": t // n_sub, "sub": lax.rem(t, n_sub)}

    og_copy = pltpu.make_async_copy(og_any, og, loc_sem.at[4])
    pa_copy = pltpu.make_async_copy(pa_any, pa, loc_sem.at[5])
    list_copies = [
        pltpu.make_async_copy(source, kept, loc_sem.at[6 + i])
        for i, (source, kept) in enumerate(((tr_any, tr), (tc_any, tc), (cnt_any, cnt)))
    ]
    og_copy.start()
    pa_copy.start()
    for copy in list_copies:
        copy.start()

    barrier = pltpu.get_barrier_semaphore()
    for o in range(1, n):
        pl.semaphore_signal(barrier, inc=1, device_id={"blk": lax.rem(b + o, n)}, device_id_type=MESH)
    for o in range(1, members):
        pl.semaphore_signal(barrier, inc=1, device_id=member(lax.rem(m + o, members)), device_id_type=MESH)

    tiles_copy = pltpu.make_async_copy(tiles_any, tiles.at[pl.ds(0, slots)], loc_sem.at[0])
    feat_copy = pltpu.make_async_copy(feat_any, feat, loc_sem.at[1])
    w_copy = pltpu.make_async_copy(w_any, w, loc_sem.at[2])
    tiles_copy.start()
    feat_copy.start()
    w_copy.start()

    og_copy.wait()
    pa_copy.wait()
    for c in range(halves):
        cols = pl.ds(c * HALF, HALF)
        x = og[:, cols]
        gath[b, c] = jnp.where(pa[:, cols] > 0, x, jnp.zeros_like(x))

    def block_copy(c, p, origin, way):
        at = pl.ds(p * span, span)
        return pltpu.make_async_remote_copy(
            src_ref=gath.at[origin, c, at], dst_ref=gath.at[origin, c, at],
            send_sem=ssem.at[way, origin, c, p], recv_sem=rsem.at[origin, c, p],
            device_id={"blk": jnp.clip(b + (1 if way else -1), 0, n - 1)}, device_id_type=MESH)

    def send(c, p, origin, way):
        @pl.when((b + 1 < n) if way else (b > 0))
        def _():
            block_copy(c, p, origin, way).start()

    def send_own(c):
        for p in range(PIECES):
            send(c, p, b, 0)
            send(c, p, b, 1)

    def feat_send(o):
        return pltpu.make_async_remote_copy(
            src_ref=feat_t.at[m], dst_ref=feat_t.at[m],
            send_sem=ft_ss.at[o - 1], recv_sem=ft_rs.at[m],
            device_id=member(lax.rem(m + o, members)), device_id_type=MESH)

    def feat_recv(o):
        origin = lax.rem(m + o, members)
        return pltpu.make_async_remote_copy(
            src_ref=feat_t.at[origin], dst_ref=feat_t.at[origin],
            send_sem=ft_ss.at[o - 1], recv_sem=ft_rs.at[origin],
            device_id=member(origin), device_id_type=MESH)

    pl.semaphore_wait(barrier, n - 1 + members - 1)
    send_own(0)
    feat_copy.wait()
    feat_t[m] = feat[...].T
    for o in range(1, members):
        feat_send(o).start()

    for copy in list_copies:
        copy.wait()

    lane = lax.broadcasted_iota(jnp.int32, (1, inv_v.shape[1]), 1)

    def invert(g, carry):
        v = jnp.full((1, inv_v.shape[1]), slots, jnp.int32)
        for k in range(CAP):
            slot = g * CAP + k
            key = jnp.where(k < cnt[g], tr[slot] * shard + tc[slot], -1)
            v = jnp.where(lane == key, slot, v)
        inv_v[pl.ds(g, 1), :] = v
        return carry

    lax.fori_loop(0, n, invert, 0)
    inv_copy = pltpu.make_async_copy(inv_v, inv_s, loc_sem.at[3])
    inv_copy.start()
    tiles[slots] = jnp.zeros((TILE, TILE), BF16)
    inv_copy.wait()
    tiles_copy.wait()

    def build(g):
        where = g if keep else 0

        def one(t, carry):
            for c in range(shard):
                index = inv_s[g, t * shard + c]
                dense[where, pl.ds(pl.multiple_of(t * TILE, TILE), TILE), pl.ds(c * TILE, TILE)] = tiles[index]
            return carry

        lax.fori_loop(0, strip_tiles, one, 0)

    def accumulate(g, c, first):
        where = g if keep else 0
        if c == 0 or not keep:
            build(g)
        step = 512

        def one(t, carry):
            at = pl.ds(pl.multiple_of(t * step, step), step)
            product = jnp.dot(dense[where, at, :], gath[g, c], preferred_element_type=F32)
            if first:
                part[c, at, :] = product
            else:
                part[c, at, :] += product
            return carry

        lax.fori_loop(0, strip // step, one, 0)

    def gather(c, low, high):
        def one(d, carry):
            for p in range(PIECES):
                @pl.when(b - d >= 0)
                def _():
                    block_copy(c, p, b - d, 1).wait_recv()
                    send(c, p, b - d, 1)

                @pl.when(b + d < n)
                def _():
                    block_copy(c, p, b + d, 0).wait_recv()
                    send(c, p, b + d, 0)

            if c + 1 < halves:
                @pl.when(d == 1)
                def _():
                    send_own(c + 1)

            @pl.when(b - d >= 0)
            def _():
                accumulate(b - d, c, False)

            @pl.when(b + d < n)
            def _():
                accumulate(b + d, c, False)
            return carry

        if low < high:
            lax.fori_loop(low, high, one, 0)

    def sub_copy(c, o, q):
        at = pl.ds(pl.multiple_of(q * rows, rows), rows)
        return pltpu.make_async_remote_copy(
            src_ref=sub_out.at[c, o - 1, at], dst_ref=sub_in.at[c, o - 1, at],
            send_sem=sub_ss.at[c, o - 1, q], recv_sem=sub_rs.at[c, o - 1, q],
            device_id={"sub": lax.rem(s + o, n_sub)}, device_id_type=MESH)

    def rep_copy(c, o):
        return pltpu.make_async_remote_copy(
            src_ref=rep_out.at[c, o - 1], dst_ref=rep_in.at[c, o - 1],
            send_sem=rep_ss.at[c, o - 1], recv_sem=rep_rs.at[c, o - 1],
            device_id={"rep": lax.rem(r + o, n_rep)}, device_id_type=MESH)

    def block_rows(t):
        return pl.ds(pl.multiple_of(t * rows, rows), rows)

    def sub_stage(c):
        for p in range(1, n_rep + 1):
            q = lax.rem(r + p, n_rep)
            for o in range(1, n_sub):
                t = lax.rem(s + o, n_sub)
                sub_out[c, o - 1, block_rows(q), :] = part[c, block_rows(q * n_sub + t), :].astype(SUB_WIRE)
                sub_copy(c, o, q).start()

    def rep_stage(c):
        def summed(t):
            total = part[c, block_rows(t * n_sub + s), :]
            for o in range(1, n_sub):
                sub_copy(c, o, t).wait_recv()
                total = total + sub_in[c, o - 1, block_rows(t), :].astype(F32)
            return total

        for o in range(1, n_rep):
            rep_out[c, o - 1] = summed(lax.rem(r + o, n_rep)).astype(BF16)
            rep_copy(c, o).start()
        acc[c] = summed(r)

    def prop_stage(c):
        total = acc[c]
        for o in range(1, n_rep):
            rep_copy(c, o).wait_recv()
            total = total + rep_in[c, o - 1].astype(F32)
        prop[c] = total.astype(BF16)

    def g1_copy(c, o):
        return pltpu.make_async_remote_copy(
            src_ref=g1_out.at[c, lax.rem(m + o, members)], dst_ref=g1_in.at[c, o - 1],
            send_sem=g1_ss.at[c, o - 1], recv_sem=g1_rs.at[c, o - 1],
            device_id=member(lax.rem(m + o, members)), device_id_type=MESH)

    def z_copy(c, o, origin):
        return pltpu.make_async_remote_copy(
            src_ref=zbuf.at[c, origin], dst_ref=zbuf.at[c, origin],
            send_sem=z_ss.at[c, o - 1], recv_sem=z_rs.at[c, origin],
            device_id={"blk": lax.rem(b + o, n)}, device_id_type=MESH)

    def f_copy(c, o, origin):
        return pltpu.make_async_remote_copy(
            src_ref=gfin.at[c, origin], dst_ref=gfin.at[c, origin],
            send_sem=f_ss.at[c, o - 1], recv_sem=f_rs.at[c, origin],
            device_id=member(lax.rem(m + o, members)), device_id_type=MESH)

    def weight_term(c):
        if c == 0:
            for o in range(1, members):
                feat_recv(o).wait_recv()
        total = None
        for q in range(members):
            part_b[...] = part[c, pl.ds(q * rows, rows), :].astype(BF16)
            term = jnp.dot(feat_t[q], part_b[...], preferred_element_type=F32)
            total = term if total is None else total + term
        for q in range(members):
            g1_out[c, q] = total[q * piece:(q + 1) * piece].astype(G_WIRE)
        for o in range(1, members):
            g1_copy(c, o).start()

    def strips_stage(c):
        total = g1_out[c, m].astype(F32)
        for o in range(1, members):
            g1_copy(c, o).wait_recv()
            total = total + g1_in[c, o - 1].astype(F32)
        zbuf[c, b] = total.astype(G_WIRE)
        for o in range(1, n):
            z_copy(c, o, b).start()

    def back_stage(c):
        for o in range(1, n):
            z_copy(c, o, lax.rem(b + o, n)).wait_recv()
        total = zbuf[c, 0].astype(F32)
        for q in range(1, n):
            total = total + zbuf[c, q].astype(F32)
        gfin[c, m] = total.astype(G_WIRE)
        for o in range(1, members):
            f_copy(c, o, m).start()

    def weight_out(c):
        for o in range(1, members):
            f_copy(c, o, lax.rem(m + o, members)).wait_recv()
        for q in range(members):
            gw[pl.ds(q * piece, piece), pl.ds(c * HALF, HALF)] = gfin[c, q].astype(F32)

    def feature_out():
        total = None
        for c in range(halves):
            term = lax.dot_general(prop[c], w[:, pl.ds(c * HALF, HALF)], (((1,), (1,)), ((), ())),
                                   preferred_element_type=F32)
            total = term if total is None else total + term
        fg[...] = total.astype(BF16)

    accumulate(b, 0, True)
    gather(0, 1, n)
    for c in range(halves):
        sub_stage(c)
        weight_term(c)
        if c + 1 < halves:
            accumulate(b, c + 1, True)
            gather(c + 1, 1, 2)
            rep_stage(c)
            strips_stage(c)
            gather(c + 1, 2, 3)
            prop_stage(c)
            back_stage(c)
            gather(c + 1, 3, n)
        else:
            rep_stage(c)
            strips_stage(c)
            prop_stage(c)
            w_copy.wait()
            feature_out()
            back_stage(c)
        if c > 0:
            weight_out(c - 1)
    weight_out(halves - 1)

    def drain(origin, carry):
        for c in range(halves):
            for p in range(PIECES):
                @pl.when((origin <= b) & (b + 1 < n))
                def _():
                    block_copy(c, p, origin, 1).wait_send()

                @pl.when((origin >= b) & (b > 0))
                def _():
                    block_copy(c, p, origin, 0).wait_send()
        return carry

    lax.fori_loop(0, n, drain, 0)
    for o in range(1, members):
        feat_send(o).wait_send()
    for c in range(halves):
        for o in range(1, n_sub):
            for q in range(n_rep):
                sub_copy(c, o, q).wait_send()
        for o in range(1, n_rep):
            rep_copy(c, o).wait_send()
        for o in range(1, members):
            g1_copy(c, o).wait_send()
            f_copy(c, o, m).wait_send()
        for o in range(1, n):
            z_copy(c, o, b).wait_send()


def local(n, n_rep, n_sub, out_grad, pre_act, features, weight, prop_tiles, tile_rows, tile_cols, tile_counts):
    rows, width = out_grad.shape
    f_in = features.shape[1]
    slots = prop_tiles.shape[0]
    halves = width // HALF
    members = n_rep * n_sub
    strip = members * rows
    keep = n * strip * rows * 2 <= KEEP_BYTES
    lanes = -(-(strip // TILE) * (rows // TILE) // 128) * 128
    inv_shape = (-(-n // 8) * 8, lanes)
    piece = f_in // members
    dma = pltpu.SemaphoreType.DMA
    vmem = pl.BlockSpec(memory_space=pltpu.VMEM)
    hbm = pl.BlockSpec(memory_space=pltpu.HBM)
    subs, reps = max(n_sub - 1, 1), max(n_rep - 1, 1)
    return pl.pallas_call(
        functools.partial(kernel, n, n_rep, n_sub, halves, keep),
        out_shape=(
            jax.ShapeDtypeStruct((rows, weight.shape[0]), BF16),
            jax.ShapeDtypeStruct((f_in, width), F32),
        ),
        in_specs=[hbm] * 8,
        out_specs=(vmem, vmem),
        scratch_shapes=[
            pltpu.VMEM(out_grad.shape, BF16),
            pltpu.VMEM(pre_act.shape, BF16),
            pltpu.SMEM(tile_rows.shape, jnp.int32),
            pltpu.SMEM(tile_cols.shape, jnp.int32),
            pltpu.SMEM(tile_counts.shape, jnp.int32),
            pltpu.VMEM((n, halves, rows, HALF), BF16),
            pltpu.VMEM((n if keep else 1, strip, rows), BF16),
            pltpu.VMEM((slots + 1, TILE, TILE), BF16),
            pltpu.VMEM(inv_shape, jnp.int32),
            pltpu.SMEM(inv_shape, jnp.int32),
            pltpu.VMEM((halves, strip, HALF), F32),
            pltpu.VMEM((halves, subs, n_rep * rows, HALF), SUB_WIRE),
            pltpu.VMEM((halves, subs, n_rep * rows, HALF), SUB_WIRE),
            pltpu.VMEM((halves, reps, rows, HALF), BF16),
            pltpu.VMEM((halves, reps, rows, HALF), BF16),
            pltpu.VMEM((halves, rows, HALF), F32),
            pltpu.VMEM((halves, rows, HALF), BF16),
            pltpu.VMEM(features.shape, BF16),
            pltpu.VMEM((members, f_in, rows), BF16),
            pltpu.VMEM(weight.shape, BF16),
            pltpu.VMEM((rows, HALF), BF16),
            pltpu.VMEM((halves, members, piece, HALF), G_WIRE),
            pltpu.VMEM((halves, members - 1, piece, HALF), G_WIRE),
            pltpu.VMEM((halves, n, piece, HALF), G_WIRE),
            pltpu.VMEM((halves, members, piece, HALF), G_WIRE),
            dma((9,)),
            dma((2, n, halves, PIECES)),
            dma((n, halves, PIECES)),
            dma((halves, subs, n_rep)),
            dma((halves, subs, n_rep)),
            dma((halves, reps)),
            dma((halves, reps)),
            dma((members - 1,)),
            dma((members,)),
            dma((halves, members - 1)),
            dma((halves, members - 1)),
            dma((halves, n - 1)),
            dma((halves, n)),
            dma((halves, members - 1)),
            dma((halves, members)),
        ],
        compiler_params=pltpu.CompilerParams(
            collective_id=0, has_side_effects=True, vmem_limit_bytes=64 << 20),
    )(out_grad, pre_act, tile_rows, tile_cols, tile_counts, features, weight, prop_tiles)


def solution(mesh):
    placed = P(("groups", "blk", "rep", "sub"))
    return jax.shard_map(
        functools.partial(local, mesh.shape["blk"], mesh.shape["rep"], mesh.shape["sub"]),
        mesh=mesh,
        in_specs=(placed, placed, placed, P(), placed, placed, placed, placed),
        out_specs=(placed, P("groups", None)),
        check_vma=False,
    )
```

time: 55.2 us -> 44.5 us (0.81)
  local copies, waits for them, and re-layouts: 8.71 us -> 3.34 us
  Pallas kernels: 45.6 us -> 40.3 us
    unnamed x18 -> x2, local copies, waits for them, and re-layouts: 8.71 us -> 3.34 us
    pallas_call x1, Pallas kernels: 45.6 us -> 40.3 us  [local(): pl.pallas_call(functools.partial(kernel, n, n_rep, n_sub, halves, keep),...]
where the time goes in v2:
time: 44.5 us; the launch traced here: 44.3 us
  Pallas kernels  40.3 us (91%)
  local copies, waits for them, and re-layouts  3.34 us (8%)
  between operations  0.64 us (1%)
    pallas_call x1, Pallas kernels, local(): pl.pallas_call(functools.partial(kernel, n, n_rep, n_sub, halves, keep),...  40.3 us
    unnamed x2, local copies, waits for them, and re-layouts  3.34 us

profile of v2, /device:TPU:0, one launch (start us, length us, event | category | flops | bytes accessed | tf_op | source)
XLA Modules:
  0.0 44.3 jit_solution(7965962809795972547)
XLA Ops:
  0.6 40.3 %shard_map.95 = (bf16[512,256]{1,0:T(8,128)(2,1)}, f32[256,256]{1,0:T(8,128)}) custom-call(bf16[512,256]{1,0:T(8,128)(2,1)} %og_any.1, bf16[512,256]{1,0:T(8,128)(2,1)} %pa_any.1, s32[64]{0:T(128)} %tr_any.1, s32[64]{0:T(128)} %tc_any.1, s32[4]{0:T(128)} %cnt_any.1, bf16[512,256]{1,0:T(8,128)(2,1)} %feat_any.1, bf16[256,256]{1,0:T(8,128)(2,1)} %w_any.1, ...), custom_call_target="tpu_custom_call" | custom-call | tf_op jit(solution)/shard_map/pallas_call | solution.py:369
  41.0 1.7 %copy.12 = bf16[512,256]{1,0:T(8,128)(2,1)} copy(bf16[512,256]{1,0:T(8,128)(2,1)} %get-tuple-element.4) | data formatting | bytes 524288
  42.6 1.7 %copy.13 = f32[256,256]{1,0:T(8,128)} copy(f32[256,256]{1,0:T(8,128)} %get-tuple-element.5) | data formatting | bytes 524288

commit v3 on v2

--- a/solution.py
+++ b/solution.py
@@ -17,14 +17,15 @@
 G_WIRE = jnp.bfloat16
 KEEP_BYTES = 16 << 20
 PIECES = 2
+STEP = 2048
 
 
 def kernel(n, n_rep, n_sub, halves, keep,
-           og_any, pa_any, tr_any, tc_any, cnt_any, feat_any, w_any, tiles_any,
-           fg, gw,
+           og_any, pa_any, tr_any, tc_any, cnt_any, feat_any, tiles_any,
+           prop, weight_sums,
            og, pa, tr, tc, cnt,
-           gath, dense, tiles, inv_v, inv_s, part, sub_out, sub_in, rep_out, rep_in, acc, prop,
-           feat, feat_t, w, part_b, g1_out, g1_in, zbuf, gfin,
+           gath, dense, tiles, inv_v, inv_s, part, sub_out, sub_in, rep_out, rep_in, acc,
+           feat, feat_t, part_b, g1_out, g1_in, zbuf, gfin,
            loc_sem, ssem, rsem, sub_ss, sub_rs, rep_ss, rep_rs, ft_ss, ft_rs, g1_ss, g1_rs, z_ss, z_rs, f_ss, f_rs):
     rows = og_any.shape[0]
     slots = tiles_any.shape[0]
@@ -61,10 +62,8 @@
 
     tiles_copy = pltpu.make_async_copy(tiles_any, tiles.at[pl.ds(0, slots)], loc_sem.at[0])
     feat_copy = pltpu.make_async_copy(feat_any, feat, loc_sem.at[1])
-    w_copy = pltpu.make_async_copy(w_any, w, loc_sem.at[2])
     tiles_copy.start()
     feat_copy.start()
-    w_copy.start()
 
     og_copy.wait()
     pa_copy.wait()
@@ -146,10 +145,9 @@
         where = g if keep else 0
         if c == 0 or not keep:
             build(g)
-        step = 512
 
         def one(t, carry):
-            at = pl.ds(pl.multiple_of(t * step, step), step)
+            at = pl.ds(pl.multiple_of(t * STEP, STEP), STEP)
             product = jnp.dot(dense[where, at, :], gath[g, c], preferred_element_type=F32)
             if first:
                 part[c, at, :] = product
@@ -157,7 +155,7 @@
                 part[c, at, :] += product
             return carry
 
-        lax.fori_loop(0, strip // step, one, 0)
+        lax.fori_loop(0, strip // STEP, one, 0)
 
     def gather(c, low, high):
         def one(d, carry):
@@ -231,7 +229,7 @@
         for o in range(1, n_rep):
             rep_copy(c, o).wait_recv()
             total = total + rep_in[c, o - 1].astype(F32)
-        prop[c] = total.astype(BF16)
+        prop[:, pl.ds(c * HALF, HALF)] = total.astype(BF16)
 
     def g1_copy(c, o):
         return pltpu.make_async_remote_copy(
@@ -288,40 +286,29 @@
         for o in range(1, members):
             f_copy(c, o, lax.rem(m + o, members)).wait_recv()
         for q in range(members):
-            gw[pl.ds(q * piece, piece), pl.ds(c * HALF, HALF)] = gfin[c, q].astype(F32)
-
-    def feature_out():
-        total = None
-        for c in range(halves):
-            term = lax.dot_general(prop[c], w[:, pl.ds(c * HALF, HALF)], (((1,), (1,)), ((), ())),
-                                   preferred_element_type=F32)
-            total = term if total is None else total + term
-        fg[...] = total.astype(BF16)
+            weight_sums[pl.ds(q * piece, piece), pl.ds(c * HALF, HALF)] = gfin[c, q]
 
     accumulate(b, 0, True)
     gather(0, 1, n)
     for c in range(halves):
         sub_stage(c)
         weight_term(c)
+        if c > 0:
+            back_stage(c - 1)
         if c + 1 < halves:
             accumulate(b, c + 1, True)
-            gather(c + 1, 1, 2)
+            gather(c + 1, 1, 3)
             rep_stage(c)
             strips_stage(c)
-            gather(c + 1, 2, 3)
-            prop_stage(c)
-            back_stage(c)
             gather(c + 1, 3, n)
         else:
             rep_stage(c)
             strips_stage(c)
-            prop_stage(c)
-            w_copy.wait()
-            feature_out()
             back_stage(c)
-        if c > 0:
-            weight_out(c - 1)
-    weight_out(halves - 1)
+            for q in range(halves):
+                prop_stage(q)
+    for c in range(halves):
+        weight_out(c)
 
     def drain(origin, carry):
         for c in range(halves):
@@ -349,6 +336,12 @@
             f_copy(c, o, m).wait_send()
         for o in range(1, n):
             z_copy(c, o, b).wait_send()
+
+
+def finish(prop, w, weight_sums, fg, gw):
+    fg[...] = lax.dot_general(prop[...], w[...], (((1,), (1,)), ((), ())),
+                              preferred_element_type=F32).astype(BF16)
+    gw[...] = weight_sums[...].astype(F32)
 
 
 def local(n, n_rep, n_sub, out_grad, pre_act, features, weight, prop_tiles, tile_rows, tile_cols, tile_counts):
@@ -366,13 +359,13 @@
     vmem = pl.BlockSpec(memory_space=pltpu.VMEM)
     hbm = pl.BlockSpec(memory_space=pltpu.HBM)
     subs, reps = max(n_sub - 1, 1), max(n_rep - 1, 1)
-    return pl.pallas_call(
+    prop, weight_sums = pl.pallas_call(
         functools.partial(kernel, n, n_rep, n_sub, halves, keep),
         out_shape=(
-            jax.ShapeDtypeStruct((rows, weight.shape[0]), BF16),
-            jax.ShapeDtypeStruct((f_in, width), F32),
+            jax.ShapeDtypeStruct((rows, width), BF16),
+            jax.ShapeDtypeStruct((f_in, width), G_WIRE),
         ),
-        in_specs=[hbm] * 8,
+        in_specs=[hbm] * 7,
         out_specs=(vmem, vmem),
         scratch_shapes=[
             pltpu.VMEM(out_grad.shape, BF16),
@@ -391,10 +384,8 @@
             pltpu.VMEM((halves, reps, rows, HALF), BF16),
             pltpu.VMEM((halves, reps, rows, HALF), BF16),
             pltpu.VMEM((halves, rows, HALF), F32),
-            pltpu.VMEM((halves, rows, HALF), BF16),
             pltpu.VMEM(features.shape, BF16),
             pltpu.VMEM((members, f_in, rows), BF16),
-            pltpu.VMEM(weight.shape, BF16),
             pltpu.VMEM((rows, HALF), BF16),
             pltpu.VMEM((halves, members, piece, HALF), G_WIRE),
             pltpu.VMEM((halves, members - 1, piece, HALF), G_WIRE),
@@ -418,7 +409,16 @@
         ],
         compiler_params=pltpu.CompilerParams(
             collective_id=0, has_side_effects=True, vmem_limit_bytes=64 << 20),
-    )(out_grad, pre_act, tile_rows, tile_cols, tile_counts, features, weight, prop_tiles)
+    )(out_grad, pre_act, tile_rows, tile_cols, tile_counts, features, prop_tiles)
+    return pl.pallas_call(
+        finish,
+        out_shape=(
+            jax.ShapeDtypeStruct((rows, weight.shape[0]), BF16),
+            jax.ShapeDtypeStruct((f_in, width), F32),
+        ),
+        in_specs=[vmem] * 3,
+        out_specs=(vmem, vmem),
+    )(prop, weight, weight_sums)
 
 
 def solution(mesh):

time: 44.5 us -> 40.2 us (0.903)
  local copies, waits for them, and re-layouts: 3.34 us -> 0 us
  Pallas kernels: 40.3 us -> 39.4 us
    unnamed x2 -> x0, local copies, waits for them, and re-layouts: 3.34 us -> none
    pallas_call x1, Pallas kernels: 40.3 us -> 37.4 us  [local(): pl.pallas_call(functools.partial(kernel, n, n_rep, n_sub, halves, keep),...]
    pallas_call x0 -> x1, Pallas kernels: none -> 2.03 us  [local(): pl.pallas_call(finish, out_shape=(jax.ShapeDtypeStruct((rows, weight.shap...]
where the time goes in v3:
time: 40.2 us; the launch traced here: 40.1 us
  Pallas kernels  39.4 us (98%)
  between operations  0.64 us (2%)
    pallas_call x1, Pallas kernels, local(): pl.pallas_call(functools.partial(kernel, n, n_rep, n_sub, halves, keep),...  37.4 us
    pallas_call x1, Pallas kernels, local(): pl.pallas_call(finish, out_shape=(jax.ShapeDtypeStruct((rows, weight.shap...  2.03 us

profile of v3, /device:TPU:0, one launch (start us, length us, event | category | flops | bytes accessed | tf_op | source)
XLA Modules:
  0.0 40.1 jit_solution(6109402901079861342)
XLA Ops:
  0.6 37.4 %shard_map.95 = (bf16[512,256]{1,0:T(8,128)(2,1)}, bf16[256,256]{1,0:T(8,128)(2,1)}) custom-call(bf16[512,256]{1,0:T(8,128)(2,1)} %og_any.1, bf16[512,256]{1,0:T(8,128)(2,1)} %pa_any.1, s32[64]{0:T(128)} %tr_any.1, s32[64]{0:T(128)} %tc_any.1, s32[4]{0:T(128)} %cnt_any.1, bf16[512,256]{1,0:T(8,128)(2,1)} %feat_any.1, bf16[64,128,128]{2,1,0:T(8,128)(2,1)} %tiles_any.1), custom_call_target="tpu_custom_call" | custom-call | tf_op jit(solution)/shard_map/pallas_call | solution.py:362
  38.0 2.0 %shard_map.96 = (bf16[512,256]{1,0:T(8,128)(2,1)}, f32[256,256]{1,0:T(8,128)}) custom-call(bf16[512,256]{1,0:T(8,128)(2,1)} %get-tuple-element.4.prop, bf16[256,256]{1,0:T(8,128)(2,1)} %w.1, bf16[256,256]{1,0:T(8,128)(2,1)} %get-tuple-element.5.weight_sums), custom_call_target="tpu_custom_call" | custom-call | tf_op jit(solution)/shard_map/pallas_call | solution.py:413
